TPU v7x, 256 devices: a whole 4x4x8 slice. The times are simulated.
256 devices in a mesh: loop: 16 (over y_hi, z), grp: 16 (over y_lo, x, core).
Axes of the slice: x: 4, y: 4 (y_hi: 2, y_lo: 2; y = y_hi * 2 + y_lo), z: 8, core: 2. Of those that a mesh axis runs over, the one named last changes fastest.
Arguments:
- queries: bfloat16 [24576, 1024], P(('loop', 'grp')), may hold values from -3 to 3
- passages: bfloat16 [24576, 1024], P(('grp', 'loop')), may hold values from -3 to 3
- pair: int32 [24576], P(('loop', 'grp')), may hold values from 0 to 24575, each once
Outputs:
- query_grad: bfloat16 [24576, 1024], P(('loop', 'grp'))
- passage_grad: bfloat16 [24576, 1024], P(('grp', 'loop'))
- loss: float32 [], replicated
Inputs may be any that keep to these rules, and one draw needn't show every extreme that they name: `pair`: every passage is the positive of exactly one query.
All inputs are finite; a program needn't handle non-finite values.
Results may differ from a plain program's by a relative error of at most 0.0031.
Values may be sent and summed in bfloat16 or wider, within the bound.
A program may use at most 64 MiB of HBM per device.

v0:
```python
import functools
import math

import jax
import jax.numpy as jnp
from jax import lax
from jax.experimental import pallas as pl
from jax.experimental.pallas import tpu as pltpu
from jax.sharding import PartitionSpec as P

MESH = pl.DeviceIdType.MESH
D = 1024
OWN = 96
HALF = 48
ROWS = 1536
BUNDLE = 192
CHUNK = 384
COLS = 512
PAIRS = 24576
TO_LOG2 = 50.0 * math.log2(math.e)
LN2 = math.log(2.0)
GRAD_SCALE = 25.0
LEVELS = 32000.0
SMALLEST = 1e-30
LOWEST = -1e38
RING4 = (0, 1, -1, 2)
RING8 = (0, 1, -1, 2, -2, 3, -3, 4)
AT4 = {0: 0, 1: 1, -1: 2, 2: 3}
AT8 = {0: 0, 1: 1, -1: 2, 2: 3, -2: 4, 3: 5, -3: 6, 4: 7}
MESSAGES = 144
f32 = jnp.float32
bf16 = jnp.bfloat16
i16 = jnp.int16


def tiles(rows, cols):
    return (rows // 16) * (cols // 128) + 1


def kernel(
    q_in, p_in, pair_in, qg_out, pg_out, loss_out,
    q_all, p_all, pair_own, scores, w,
    row_peak, row_sum, col_peak, col_sum,
    row_stats, col_stats, row_lse, row_rep, pair_rep, order, col_lse, col_rep, col_index,
    term, sib, far_out, far_in, near_out, near_in, rest_out, rest_in, last_out, last_in,
    z_far_out, z_far_in, z_out, z_in, loss_out_buf, loss_in_buf, positive,
    send_sem, recv_sem, own_sem,
):
    loop = lax.axis_index("loop")
    grp = lax.axis_index("grp")
    core = lax.rem(grp, 2)
    x = lax.rem(lax.div(grp, 2), 4)
    y = lax.div(loop, 8) * 2 + lax.div(grp, 8)
    z = lax.rem(loop, 8)

    xs = [x] + [lax.rem(x + d, 4) for d in (1, 2, 3)]
    ys = [y] + [lax.rem(y + d, 4) for d in (1, 2, 3)]
    zs8 = [z] + [lax.rem(z + d, 8) for d in range(1, 8)]
    cores = [core, 1 - core]
    y_loop = [lax.div(v, 2) * 8 for v in ys]
    y_grp = [lax.rem(v, 2) * 8 for v in ys]

    def device(dx=0, dy=0, dz=0, dc=0):
        return {
            "loop": y_loop[dy % 4] + zs8[dz % 8],
            "grp": y_grp[dy % 4] + xs[dx % 4] * 2 + cores[dc],
        }

    def hops(d, size):
        return min(d, size - d)

    plane = [(dx, dy) for dx in range(4) for dy in range(4) if dx or dy]
    plane.sort(key=lambda d: -hops(d[0], 4) - hops(d[1], 4))
    column = [(dz, dc) for dz in range(8) for dc in range(2) if dz or dc]
    column.sort(key=lambda d: -hops(d[0], 8) * 2 - d[1])

    barrier = pltpu.get_barrier_semaphore()
    neighbours = [{"dx": 1}, {"dx": -1}, {"dy": 1}, {"dy": -1}, {"dz": 1}, {"dz": -1}, {"dc": 1}]
    for where in neighbours:
        pl.semaphore_signal(barrier, inc=1, device_id=device(**where), device_id_type=MESH)
    own = [
        pltpu.make_async_copy(src, dst, own_sem.at[k])
        for k, (src, dst) in enumerate(
            (
                (q_in.at[pl.ds(0, HALF), :], q_all.at[pl.ds(0, HALF), :]),
                (q_in.at[pl.ds(HALF, HALF), :], q_all.at[pl.ds(BUNDLE, HALF), :]),
                (p_in, p_all.at[pl.ds(0, OWN), :]),
                (pair_in, pair_own),
            )
        )
    ]
    for copy in own:
        copy.start()

    count = [0]
    sent = []

    def send(src, dst, **where):
        k = count[0]
        count[0] += 1
        copy = pltpu.make_async_remote_copy(
            src_ref=src, dst_ref=dst, send_sem=send_sem.at[k], recv_sem=recv_sem.at[k],
            device_id=device(**where), device_id_type=MESH,
        )
        copy.start()
        sent.append(copy)
        return copy

    def q_at(half, p, q, cols=(0, D)):
        return q_all.at[pl.ds((2 * p + half) * BUNDLE + q * HALF, HALF), pl.ds(*cols)]

    def p_at(pos, rel, h=None):
        start = pos * BUNDLE + rel * OWN
        if h is None:
            return p_all.at[pl.ds(start, OWN), :]
        return p_all.at[pl.ds(start + h * HALF, HALF), :]

    pl.semaphore_wait(barrier, len(neighbours))
    for copy in own:
        copy.wait()

    first_axis, second_axis = ("dx", "dy"), ("dy", "dx")
    zs, near1, far1, near2, far2, sibling = {}, {}, {}, {}, {}, {}

    def spread(half, q):
        for sign in (1, -1):
            near2[half, sign, q] = send(
                q_at(half, 0, q), q_at(half, AT4[-sign], q), **{second_axis[half]: sign}
            )

    def z_own(h):
        for sign in (1, -1):
            zs[sign, 1, h] = send(p_at(0, 0, h), p_at(AT8[-sign], 0, h), dz=sign)

    def z_pass(k, h):
        for sign in (1, -1):
            last = h != (0 if sign == 1 else 1)
            if k == 4 and last:
                continue
            zs[sign, k, h].wait_recv()
            if k < 3 or (k == 3 and not last):
                pos, to = AT8[-sign * k], AT8[-sign * (k + 1)] if k < 3 else 7
                zs[sign, k + 1, h] = send(p_at(pos, 0, h), p_at(to, 0, h), dz=sign)

    def to_sibling(*positions):
        for pos in positions:
            sibling[pos] = send(p_at(pos, 0), p_at(pos, 1), dc=1)

    def pass_far(q):
        for half in (0, 1):
            for sign in (1, -1):
                near2[half, sign, q].wait_recv()
                if (q < 2) == (sign == 1):
                    far2[half, q] = send(
                        q_at(half, AT4[-sign], q), q_at(half, 3, q), **{second_axis[half]: sign}
                    )

    for half in (0, 1):
        for sign in (1, -1):
            near1[half, sign] = send(q_at(half, 0, 0), q_at(half, 0, AT4[-sign]), **{first_axis[half]: sign})
    z_own(0)
    for half in (0, 1):
        spread(half, 0)
    z_own(1)
    to_sibling(0)
    row_peak[...] = jnp.full(row_peak.shape, LOWEST, f32)
    row_sum[...] = jnp.zeros(row_sum.shape, f32)
    col_peak[...] = jnp.full(col_peak.shape, LOWEST, f32)
    col_sum[...] = jnp.zeros(col_sum.shape, f32)
    slot = x * 4 + y
    col_slot = z * 2 + core
    row_stats[slot] = jnp.zeros((40, 128), f32)
    col_stats[col_slot] = jnp.zeros((16, 128), f32)
    row_stats[slot, pl.ds(32, 1), pl.ds(0, OWN)] = pair_own[...].astype(f32)

    z_pass(1, 0)
    for half in (0, 1):
        for sign in (1, -1):
            q = AT4[-sign]
            near1[half, sign].wait_recv()
            cols = (0, D // 2) if sign == 1 else (D // 2, D // 2)
            far1[half, sign] = send(q_at(half, 0, q, cols), q_at(half, 0, 3, cols), **{first_axis[half]: sign})
            spread(half, q)
    z_pass(1, 1)
    to_sibling(1, 2)
    pass_far(0)
    for half in (0, 1):
        for sign in (1, -1):
            far1[half, sign].wait_recv()
        spread(half, 3)
    z_pass(2, 0)

    def block(p, start, width):
        rows = pl.ds(p * CHUNK, CHUNK)
        cols = pl.ds(start, width)
        s = lax.dot_general(
            q_all[rows, :], p_all[cols, :], (((1,), (1,)), ((), ())), preferred_element_type=f32
        ) * TO_LOG2
        scores[rows, cols] = s
        parts = [s[:, 128 * i : 128 * (i + 1)] for i in range(width // 128)]
        old = row_peak[rows, :]
        peak = functools.reduce(jnp.maximum, parts, old)
        total = row_sum[rows, :] * jnp.exp2(old - peak)
        for part in parts:
            total += jnp.exp2(part - peak)
        row_peak[rows, :] = peak
        row_sum[rows, :] = total
        s3 = s.reshape(CHUNK // 8, 8, width)
        old = col_peak[:, cols]
        peak = jnp.maximum(old, jnp.max(s3, axis=0))
        col_sum[:, cols] = col_sum[:, cols] * jnp.exp2(old - peak) + jnp.sum(jnp.exp2(s3 - peak[None]), axis=0)
        col_peak[:, cols] = peak

    for pos in (0, 1, 2):
        sibling[pos].wait_recv()
    block(0, 0, 512)
    pass_far(1)
    z_pass(2, 1)
    to_sibling(3, 4)
    pass_far(2)
    z_pass(3, 0)
    pass_far(3)
    block(1, 0, 512)
    z_pass(3, 1)
    to_sibling(5, 6)
    block(2, 0, 512)
    for pos in (3, 4, 5, 6):
        sibling[pos].wait_recv()
    block(0, 512, 512)
    z_pass(4, 0)
    z_pass(4, 1)
    to_sibling(7)
    block(1, 512, 512)
    block(2, 512, 512)
    for half in (0, 1):
        for q in range(4):
            far2[half, q].wait_recv()
    block(3, 0, 1024)
    sibling[7].wait_recv()

    def piece(half, p, q):
        dx, dy = (RING4[q], RING4[p]) if half == 0 else (RING4[p], RING4[q])
        return xs[dx % 4] * 4 + ys[dy % 4]

    def owner(pos, rel):
        return zs8[RING8[pos] % 8] * 2 + cores[rel]

    def finish_rows(p):
        rows = pl.ds(p * CHUNK, CHUNK)
        lanes = row_peak[rows, :].T
        peak = jnp.max(lanes, axis=0, keepdims=True)
        total = jnp.sum(row_sum[rows, :].T * jnp.exp2(lanes - peak), axis=0, keepdims=True)
        lse = peak + jnp.log(total) * (1.0 / LN2)
        for half in (0, 1):
            for q in range(4):
                start = half * BUNDLE + q * HALF
                row_stats[slot, pl.ds(half * 16 + piece(half, p, q), 1), pl.ds(0, HALF)] = lse[:, start : start + HALF]

    block(0, 1024, 512)
    block(1, 1024, 512)
    finish_rows(0)
    block(2, 1024, 512)
    finish_rows(1)
    block(3, 1024, 512)
    finish_rows(2)
    peak = jnp.max(col_peak[...], axis=0, keepdims=True)
    total = jnp.sum(col_sum[...] * jnp.exp2(col_peak[...] - peak), axis=0, keepdims=True)
    lse = peak + jnp.log(total) * (1.0 / LN2)
    for pos in range(8):
        for rel in (0, 1):
            start = pos * BUNDLE + rel * OWN
            col_stats[col_slot, pl.ds(owner(pos, rel), 1), pl.ds(0, OWN)] = lse[:, start : start + OWN]
    finish_rows(3)
    row_msgs, col_msgs = [], []
    for (dx, dy), (dz, dc) in zip(plane, column, strict=True):
        row_msgs.append(send(row_stats.at[slot], row_stats.at[slot], dx=dx, dy=dy))
        col_msgs.append(send(col_stats.at[col_slot], col_stats.at[col_slot], dz=dz, dc=dc))

    j = lax.broadcasted_iota(jnp.int32, (1, ROWS), 1)
    part = lax.shift_right_logical(j * 683, 16)
    within = j - part * OWN
    pos = lax.shift_right_logical(part, 1)
    away = lax.shift_right_logical(pos + 1, 1)
    away = jnp.where((pos & 1) == 1, away, -away)
    z2 = (z + away + 8) & 7
    c2 = (core + part) & 1
    first = (lax.div(grp, 2) * 2 + c2) * 16 + lax.div(loop, 8) * 8 + z2
    col_index[...] = (first * OWN + within).astype(f32)

    for m in row_msgs:
        m.wait_recv()
    stats = row_stats[:, 0:32, :]
    peak = jnp.max(stats, axis=0)
    lse = peak + jnp.log(jnp.sum(jnp.exp2(stats - peak[None]), axis=0)) * (1.0 / LN2)
    row_lse[...] = lse
    lane = lax.broadcasted_iota(jnp.int32, (32, 128), 1)
    share = jnp.sum(jnp.where(lane < HALF, lse, 0.0).reshape(4, 8, 128), axis=0)
    order[pl.ds(64, 64), :] = jnp.zeros((64, 128), f32)
    for b in range(8):
        p, half = b // 2, b % 2
        for q in range(4):
            at = piece(half, p, q)
            order[pl.ds(4 * b + q, 1), :] = row_lse[pl.ds(half * 16 + at, 1), :]
            order[pl.ds(32 + 4 * b + q, 1), :] = row_stats[at, pl.ds(32, 1), :]
    turned = order[...].T
    for b in range(8):
        half = b % 2
        for q in range(4):
            n = 4 * b + q
            rows = pl.ds(n * HALF, HALF)
            row_rep[rows, :] = jnp.broadcast_to(turned[0:HALF, n : n + 1], (HALF, 128))
            pair_rep[rows, :] = jnp.broadcast_to(
                turned[half * HALF : (half + 1) * HALF, 32 + n : 33 + n], (HALF, 128)
            )

    for m in col_msgs:
        m.wait_recv()
    stats = col_stats[...]
    peak = jnp.max(stats, axis=0)
    lse = peak + jnp.log(jnp.sum(jnp.exp2(stats - peak[None]), axis=0)) * (1.0 / LN2)
    col_lse[...] = lse
    lane = lax.broadcasted_iota(jnp.int32, (16, 128), 1)
    share = share + jnp.sum(jnp.where(lane < OWN, lse, 0.0).reshape(2, 8, 128), axis=0)
    col_rep[...] = jnp.concatenate(
        [col_lse[pl.ds(owner(pos, rel), 1), :][:, 0:OWN] for pos in range(8) for rel in (0, 1)], axis=1
    )

    positive[...] = jnp.zeros((8, 128), f32)

    def weigh(p, k):
        rows, cols = pl.ds(p * CHUNK, CHUNK), pl.ds(k * CHUNK, CHUNK)
        s = scores[rows, cols]
        hit = jnp.concatenate([pair_rep[rows, :]] * 3, axis=1) == col_index[:, cols]
        weight = (
            jnp.exp2(s - jnp.concatenate([row_rep[rows, :]] * 3, axis=1))
            + jnp.exp2(s - col_rep[:, cols])
            - jnp.where(hit, 2.0, 0.0)
        )
        found = jnp.sum(jnp.where(hit, s, 0.0).reshape(CHUNK // 8, 8, CHUNK), axis=0)
        positive[...] += found[:, 0:128] + found[:, 128:256] + found[:, 256:384]
        w[rows, cols] = weight.astype(bf16)

    def query_term(p):
        rows = pl.ds(p * CHUNK, CHUNK)
        scores[rows, pl.ds(0, D)] = jnp.dot(w[rows, :], p_all[...], preferred_element_type=f32)

    def near_rows(half, s, side):
        return (1 + s) * CHUNK + half * BUNDLE + side * OWN

    def near_terms(part):
        starts = [near_rows(half, s, s if part else 1 - s) for half in (0, 1) for s in (0, 1)]
        rows = jnp.concatenate([w[pl.ds(start, OWN), :] for start in starts], axis=0)
        out = jnp.dot(rows, p_all[...], preferred_element_type=f32)
        for i, start in enumerate(starts):
            scores[pl.ds(start, OWN), pl.ds(0, D)] = out[i * OWN : (i + 1) * OWN, :]

    sib_msgs = {}

    def passage_term(k):
        rows = pl.ds(k * CHUNK, CHUNK)
        term[rows, :] = lax.dot_general(
            w[:, rows], q_all[...], (((0,), (0,)), ((), ())), preferred_element_type=f32
        )

    def sib_send(k):
        for pos in (2 * k + 1, 2 * k):
            sib_msgs[pos] = send(
                term.at[pl.ds(pos * BUNDLE + OWN, OWN), :], sib.at[pl.ds(pos * OWN, OWN), :], dc=1
            )

    def add_sibling(*positions):
        for pos in positions:
            sib_msgs[pos].wait_recv()
        for pos in positions:
            term[pl.ds(pos * BUNDLE, OWN), :] += sib[pl.ds(pos * OWN, OWN), :]

    def encode(ref, r0, rows, c0, cols, buf):
        peak = functools.reduce(
            jnp.maximum,
            [
                jnp.max(jnp.abs(ref[pl.ds(r0, rows), pl.ds(c0 + 128 * i, 128)]).reshape(rows // 8, 8, 128), axis=0)
                for i in range(cols // 128)
            ],
        )
        power = jnp.floor(jnp.log(jnp.maximum(peak, SMALLEST)) * (1.0 / LN2)) + 1.0
        factor = (jnp.exp2(-power) * LEVELS)[None]
        n = rows // 16
        for i in range(cols // 128):
            v = ref[pl.ds(r0, rows), pl.ds(c0 + 128 * i, 128)].reshape(rows // 8, 8, 128) * factor
            buf[pl.ds(i * n, n)] = jnp.round(v).astype(jnp.int32).reshape(n, 16, 128).astype(i16)
        both = jnp.concatenate([power, power], axis=0).astype(jnp.int32)
        buf[pl.ds(n * (cols // 128), 1)] = both.astype(i16)[None]

    def add_decoded(ref, r0, rows, c0, cols, buf):
        n = rows // 16
        power = buf[n * (cols // 128)].astype(jnp.int32).astype(f32)[0:8]
        factor = (jnp.exp2(power) * (1.0 / LEVELS))[None]
        for i in range(cols // 128):
            v = buf[pl.ds(i * n, n)].astype(jnp.int32).astype(f32).reshape(rows // 8, 8, 128) * factor
            ref[pl.ds(r0, rows), pl.ds(c0 + 128 * i, 128)] += v.reshape(rows, 128)

    msgs = {}
    sides = [(half, sign, s) for half in (0, 1) for sign, s in ((1, 0), (-1, 1))]

    def far_send():
        for half, _, s in sides:
            encode(scores, 3 * CHUNK + half * BUNDLE + s * OWN, OWN, 0, D, far_out.at[half, s])
        for half, sign, s in sides:
            msgs["far", half, s] = send(far_out.at[half, s], far_in.at[half, s], **{second_axis[half]: sign})

    def near_send():
        for half, _, s in sides:
            encode(scores, near_rows(half, s, 1 - s), OWN, 0, D, near_out.at[half, s])
        for half, sign, s in sides:
            msgs["near", half, s] = send(near_out.at[half, s], near_in.at[half, s], **{second_axis[half]: sign})

    def far_wait():
        for half, _, s in sides:
            msgs["far", half, s].wait_recv()

    def rest_encode():
        for half, _, s in sides:
            row = near_rows(half, s, s)
            add_decoded(scores, row, OWN, 0, D, far_in.at[half, s])
            for u in (0, 1):
                encode(scores, row + (1 - u) * HALF, HALF, 0, D, rest_out.at[half, s, u])

    def rest_send():
        for u in (0, 1):
            for half, sign, s in sides:
                msgs["rest", half, s, u] = send(
                    rest_out.at[half, s, u], rest_in.at[half, s, u], **{second_axis[half]: sign}
                )

    def near_add():
        for half, _, s in sides:
            msgs["near", half, s].wait_recv()
        for half, _, s in sides:
            add_decoded(scores, half * BUNDLE + (1 - s) * OWN, OWN, 0, D, near_in.at[half, s])

    def rest_add(u):
        for half, _, s in sides:
            msgs["rest", half, s, u].wait_recv()
        for half, _, s in sides:
            add_decoded(scores, half * BUNDLE + s * OWN + (1 - u) * HALF, HALF, 0, D, rest_in.at[half, s, u])

    def last_send(*qs):
        for half in (0, 1):
            for q in qs:
                encode(scores, half * BUNDLE + q * HALF, HALF, 0, D, last_out.at[half, q - 1])
        for q in qs:
            for half in (0, 1):
                msgs["last", half, q] = send(
                    last_out.at[half, q - 1], last_in.at[half, q - 1], **{first_axis[half]: RING4[q]}
                )

    def query_out():
        for q in (1, 3, 2):
            for half in (0, 1):
                msgs["last", half, q].wait_recv()
            for half in (0, 1):
                add_decoded(scores, half * BUNDLE, HALF, 0, D, last_in.at[half, q - 1])
        for half in (0, 1):
            rows = pl.ds(half * BUNDLE, HALF)
            qg_out[pl.ds(half * HALF, HALF), :] = (scores[rows, pl.ds(0, D)] * GRAD_SCALE).astype(bf16)

    def z_far():
        for s in (0, 1):
            encode(term, 7 * BUNDLE + s * HALF, HALF, 0, D, z_far_out.at[s])
        for sign, s in ((1, 0), (-1, 1)):
            msgs["z", 4, s] = send(z_far_out.at[s], z_far_in.at[s], dz=sign)

    def z_near(k, part):
        rows = [AT8[sign * k] * BUNDLE + (s if part else 1 - s) * HALF for sign, s in ((1, 0), (-1, 1))]
        if k < 3:
            arrived = [(msgs["z", k + 1, s, part], z_in.at[k, s, part]) for s in (0, 1)]
        else:
            arrived = [(msgs["z", 4, s], z_far_in.at[s]) for s in (0, 1)] if part else []
        for message, _ in arrived:
            message.wait_recv()
        for row, (_, buf) in zip(rows, arrived):
            add_decoded(term, row, HALF, 0, D, buf)
        for s in (0, 1):
            encode(term, rows[s], HALF, 0, D, z_out.at[k - 1, s, part])
        for sign, s in ((1, 0), (-1, 1)):
            msgs["z", k, s, part] = send(z_out.at[k - 1, s, part], z_in.at[k - 1, s, part], dz=sign)

    def passage_out():
        for part in (0, 1):
            for s in (0, 1):
                msgs["z", 1, s, part].wait_recv()
            for s in (0, 1):
                add_decoded(term, (s if part else 1 - s) * HALF, HALF, 0, D, z_in.at[0, s, part])
        pg_out[...] = (term[pl.ds(0, OWN), :] * GRAD_SCALE).astype(bf16)

    loss_slot = [0]

    def total_along(value, axis, size):
        base = loss_slot[0]
        loss_slot[0] += size
        loss_out_buf[base] = value
        copies = [
            send(loss_out_buf.at[base], loss_in_buf.at[base + d], **{axis: d}) for d in range(1, size)
        ]

        def finish():
            out = value
            for d, m in enumerate(copies, 1):
                m.wait_recv()
                out = out + loss_in_buf[base + d]
            return out

        return finish

    for p in range(4):
        weigh(p, 3)
    passage_term(3)
    for k in range(3):
        weigh(3, k)
    sib_send(3)
    query_term(3)
    for p in (1, 2):
        for k in range(3):
            weigh(p, k)
    far_send()
    add_sibling(7)
    z_far()
    near_terms(0)
    for k in (2, 1, 0):
        weigh(0, k)
    near_send()
    passage_term(2)
    sib_send(2)
    near_terms(1)
    add_sibling(5, 6)
    z_near(3, 0)
    z_near(3, 1)
    finish = total_along(share * (1.0 / 16.0) - 2.0 * positive[...], "dx", 4)
    far_wait()
    passage_term(1)
    rest_encode()
    rest_send()
    sib_send(1)
    query_term(0)
    finish = total_along(finish(), "dy", 4)
    passage_term(0)
    sib_send(0)
    add_sibling(3, 4)
    z_near(2, 0)
    near_add()
    z_near(2, 1)
    finish = total_along(finish(), "dz", 8)
    add_sibling(1, 2, 0)
    rest_add(0)
    last_send(3, 1)
    z_near(1, 0)
    rest_add(1)
    last_send(2)
    z_near(1, 1)
    finish = total_along(finish(), "dc", 2)
    total = finish()
    loss_out[...] = jnp.sum(jnp.sum(total, axis=1, keepdims=True), axis=0, keepdims=True) * (LN2 / (2.0 * PAIRS))
    query_out()
    passage_out()
    for copy in sent:
        copy.wait_send()


def on_device(queries, passages, pair):
    vmem = pl.BlockSpec(memory_space=pltpu.VMEM)
    anywhere = pl.BlockSpec(memory_space=pl.ANY)
    query_grad, passage_grad, loss = pl.pallas_call(
        kernel,
        out_shape=(
            pltpu.VMEM((OWN, D), bf16),
            pltpu.VMEM((OWN, D), bf16),
            jax.ShapeDtypeStruct((1, 1), f32),
        ),
        in_specs=[anywhere] * 3,
        out_specs=[vmem] * 3,
        scratch_shapes=[
            pltpu.VMEM((ROWS, D), bf16),
            pltpu.VMEM((ROWS, D), bf16),
            pltpu.VMEM((1, OWN), jnp.int32),
            pltpu.VMEM((ROWS, ROWS), f32),
            pltpu.VMEM((ROWS, ROWS), bf16),
            pltpu.VMEM((ROWS, 128), f32),
            pltpu.VMEM((ROWS, 128), f32),
            pltpu.VMEM((8, ROWS), f32),
            pltpu.VMEM((8, ROWS), f32),
            pltpu.VMEM((16, 40, 128), f32),
            pltpu.VMEM((16, 16, 128), f32),
            pltpu.VMEM((32, 128), f32),
            pltpu.VMEM((ROWS, 128), f32),
            pltpu.VMEM((ROWS, 128), f32),
            pltpu.VMEM((128, 128), f32),
            pltpu.VMEM((16, 128), f32),
            pltpu.VMEM((1, ROWS), f32),
            pltpu.VMEM((1, ROWS), f32),
            pltpu.VMEM((ROWS, D), f32),
            pltpu.VMEM((ROWS // 2, D), f32),
            pltpu.VMEM((2, 2, tiles(OWN, D), 16, 128), i16),
            pltpu.VMEM((2, 2, tiles(OWN, D), 16, 128), i16),
            pltpu.VMEM((2, 2, tiles(OWN, D), 16, 128), i16),
            pltpu.VMEM((2, 2, tiles(OWN, D), 16, 128), i16),
            pltpu.VMEM((2, 2, 2, tiles(HALF, D), 16, 128), i16),
            pltpu.VMEM((2, 2, 2, tiles(HALF, D), 16, 128), i16),
            pltpu.VMEM((2, 3, tiles(HALF, D), 16, 128), i16),
            pltpu.VMEM((2, 3, tiles(HALF, D), 16, 128), i16),
            pltpu.VMEM((2, tiles(HALF, D), 16, 128), i16),
            pltpu.VMEM((2, tiles(HALF, D), 16, 128), i16),
            pltpu.VMEM((3, 2, 2, tiles(HALF, D), 16, 128), i16),
            pltpu.VMEM((3, 2, 2, tiles(HALF, D), 16, 128), i16),
            pltpu.VMEM((18, 8, 128), f32),
            pltpu.VMEM((18, 8, 128), f32),
            pltpu.VMEM((8, 128), f32),
            pltpu.SemaphoreType.DMA((MESSAGES,)),
            pltpu.SemaphoreType.DMA((MESSAGES,)),
            pltpu.SemaphoreType.DMA((4,)),
        ],
        compiler_params=pltpu.CompilerParams(
            collective_id=0, has_side_effects=True, vmem_limit_bytes=60 * 1024 * 1024
        ),
    )(queries, passages, pair.reshape(1, OWN))
    return query_grad, passage_grad, loss.reshape(())


def solution(mesh):
    in_specs = (P(("loop", "grp"), None), P(("grp", "loop"), None), P(("loop", "grp")))
    out_specs = (P(("loop", "grp"), None), P(("grp", "loop"), None), P())
    return jax.shard_map(
        on_device, mesh=mesh, in_specs=in_specs, out_specs=out_specs, check_vma=False
    )
```

profile of v0, /device:TPU:2, one launch (start us, length us, event | category | flops | bytes accessed | tf_op | source)
XLA Modules:
  0.0 81.7 jit_solution(5161453733450516806)
XLA Ops:
  0.6 78.1 %shard_map.58 = (bf16[96,1024]{1,0:T(8,128)(2,1)S(1)}, bf16[96,1024]{1,0:T(8,128)(2,1)S(1)}, f32[1,1]{1,0:T(1,128)}) custom-call(bf16[96,1024]{1,0:T(8,128)(2,1)} %q_in.1, bf16[96,1024]{1,0:T(8,128)(2,1)} %p_in.1, s32[1,96]{1,0:T(1,128)} %bitcast.2), custom_call_target="tpu_custom_call" | custom-call | tf_op jit(solution)/shard_map/pallas_call | solution.py:572
  78.7 0.7 copy.9
  79.4 0.7 copy.10
where the time goes:
time: 82.2 us; the launch traced here: 81.7 us
  Pallas kernels  78.1 us (95%)
  between operations  2.33 us (3%)
  local copies, waits for them, and re-layouts  1.36 us (2%)
    pallas_call x1, Pallas kernels, on_device(): pl.pallas_call(kernel, out_shape=(pltpu.VMEM((OWN, D), bf16), pltpu.VMEM(...  78.1 us

commit v1 on v0

--- a/solution.py
+++ b/solution.py
@@ -519,40 +519,42 @@
         weigh(3, k)
     sib_send(3)
     query_term(3)
-    for p in (1, 2):
-        for k in range(3):
-            weigh(p, k)
+    for p in range(3):
+        weigh(p, 2)
     far_send()
     add_sibling(7)
     z_far()
+    passage_term(2)
+    for p in (1, 2):
+        for k in (0, 1):
+            weigh(p, k)
+    sib_send(2)
     near_terms(0)
-    for k in (2, 1, 0):
+    for k in (0, 1):
         weigh(0, k)
     near_send()
-    passage_term(2)
-    sib_send(2)
-    near_terms(1)
     add_sibling(5, 6)
     z_near(3, 0)
     z_near(3, 1)
     finish = total_along(share * (1.0 / 16.0) - 2.0 * positive[...], "dx", 4)
+    passage_term(1)
+    sib_send(1)
+    near_terms(1)
     far_wait()
-    passage_term(1)
     rest_encode()
     rest_send()
-    sib_send(1)
-    query_term(0)
+    add_sibling(3, 4)
+    z_near(2, 0)
     finish = total_along(finish(), "dy", 4)
     passage_term(0)
     sib_send(0)
-    add_sibling(3, 4)
-    z_near(2, 0)
+    z_near(2, 1)
+    query_term(0)
     near_add()
-    z_near(2, 1)
+    rest_add(0)
+    last_send(3, 1)
     finish = total_along(finish(), "dz", 8)
     add_sibling(1, 2, 0)
-    rest_add(0)
-    last_send(3, 1)
     z_near(1, 0)
     rest_add(1)
     last_send(2)

time: 82.2 us -> 81.1 us (0.987)
  Pallas kernels: 78.1 us -> 76.2 us
    pallas_call x1, Pallas kernels: 78.1 us -> 76.2 us  [on_device(): pl.pallas_call(kernel, out_shape=(pltpu.VMEM((OWN, D), bf16), pltpu.VMEM(...]
where the time goes in v1:
time: 81.1 us; the launch traced here: 79.9 us
  Pallas kernels  76.2 us (94%)
  between operations  2.33 us (3%)
  local copies, waits for them, and re-layouts  1.36 us (2%)
    pallas_call x1, Pallas kernels, on_device(): pl.pallas_call(kernel, out_shape=(pltpu.VMEM((OWN, D), bf16), pltpu.VMEM(...  76.2 us

profile of v1, /device:TPU:2, one launch (start us, length us, event | category | flops | bytes accessed | tf_op | source)
XLA Modules:
  0.0 79.9 jit_solution(15629848783415656343)
XLA Ops:
  0.6 76.2 %shard_map.58 = (bf16[96,1024]{1,0:T(8,128)(2,1)S(1)}, bf16[96,1024]{1,0:T(8,128)(2,1)S(1)}, f32[1,1]{1,0:T(1,128)}) custom-call(bf16[96,1024]{1,0:T(8,128)(2,1)} %q_in.1, bf16[96,1024]{1,0:T(8,128)(2,1)} %p_in.1, s32[1,96]{1,0:T(1,128)} %bitcast.2), custom_call_target="tpu_custom_call" | custom-call | tf_op jit(solution)/shard_map/pallas_call | solution.py:574
  76.8 0.7 copy.9
  77.5 0.7 copy.10

commit v2 on v1

--- a/solution.py
+++ b/solution.py
@@ -41,7 +41,7 @@
     q_in, p_in, pair_in, qg_out, pg_out, loss_out,
     q_all, p_all, pair_own, scores, w,
     row_peak, row_sum, col_peak, col_sum,
-    row_stats, col_stats, row_lse, row_rep, pair_rep, order, col_lse, col_rep, col_index,
+    row_stats, col_stats, row_lse, pair_all, row_rep, pair_rep, order, col_lse, col_rep, col_index,
     term, sib, far_out, far_in, near_out, near_in, rest_out, rest_in, last_out, last_in,
     z_far_out, z_far_in, z_out, z_in, loss_out_buf, loss_in_buf, positive,
     send_sem, recv_sem, own_sem,
@@ -76,6 +76,7 @@
 
     barrier = pltpu.get_barrier_semaphore()
     neighbours = [{"dx": 1}, {"dx": -1}, {"dy": 1}, {"dy": -1}, {"dz": 1}, {"dz": -1}, {"dc": 1}]
+    neighbours += [{"dx": 2}, {"dy": 2}]
     for where in neighbours:
         pl.semaphore_signal(barrier, inc=1, device_id=device(**where), device_id_type=MESH)
     own = [
@@ -106,8 +107,8 @@
         sent.append(copy)
         return copy
 
-    def q_at(half, p, q, cols=(0, D)):
-        return q_all.at[pl.ds((2 * p + half) * BUNDLE + q * HALF, HALF), pl.ds(*cols)]
+    def q_at(half, p, q):
+        return q_all.at[pl.ds((2 * p + half) * BUNDLE + q * HALF, HALF), :]
 
     def p_at(pos, rel, h=None):
         start = pos * BUNDLE + rel * OWN
@@ -159,6 +160,8 @@
         for sign in (1, -1):
             near1[half, sign] = send(q_at(half, 0, 0), q_at(half, 0, AT4[-sign]), **{first_axis[half]: sign})
     z_own(0)
+    for half in (0, 1):
+        far1[half] = send(q_at(half, 0, 0), q_at(half, 0, 3), **{first_axis[half]: 2})
     for half in (0, 1):
         spread(half, 0)
     z_own(1)
@@ -169,24 +172,21 @@
     col_sum[...] = jnp.zeros(col_sum.shape, f32)
     slot = x * 4 + y
     col_slot = z * 2 + core
-    row_stats[slot] = jnp.zeros((40, 128), f32)
+    row_stats[slot] = jnp.zeros((16, 128), f32)
     col_stats[col_slot] = jnp.zeros((16, 128), f32)
-    row_stats[slot, pl.ds(32, 1), pl.ds(0, OWN)] = pair_own[...].astype(f32)
+    for i in range(3):
+        row_stats[slot, pl.ds(i, 1), pl.ds(OWN, 32)] = pair_own[:, 32 * i : 32 * (i + 1)].astype(f32)
 
     z_pass(1, 0)
     for half in (0, 1):
         for sign in (1, -1):
-            q = AT4[-sign]
             near1[half, sign].wait_recv()
-            cols = (0, D // 2) if sign == 1 else (D // 2, D // 2)
-            far1[half, sign] = send(q_at(half, 0, q, cols), q_at(half, 0, 3, cols), **{first_axis[half]: sign})
-            spread(half, q)
+            spread(half, AT4[-sign])
     z_pass(1, 1)
     to_sibling(1, 2)
     pass_far(0)
     for half in (0, 1):
-        for sign in (1, -1):
-            far1[half, sign].wait_recv()
+        far1[half].wait_recv()
         spread(half, 3)
     z_pass(2, 0)
 
@@ -232,10 +232,12 @@
     to_sibling(7)
     block(1, 512, 512)
     block(2, 512, 512)
+    for p in range(3):
+        block(p, 1024, 256)
     for half in (0, 1):
         for q in range(4):
             far2[half, q].wait_recv()
-    block(3, 0, 1024)
+    block(3, 0, 1280)
     sibling[7].wait_recv()
 
     def piece(half, p, q):
@@ -254,14 +256,14 @@
         for half in (0, 1):
             for q in range(4):
                 start = half * BUNDLE + q * HALF
-                row_stats[slot, pl.ds(half * 16 + piece(half, p, q), 1), pl.ds(0, HALF)] = lse[:, start : start + HALF]
-
-    block(0, 1024, 512)
-    block(1, 1024, 512)
+                row_stats[slot, pl.ds(piece(half, p, q), 1), pl.ds(half * HALF, HALF)] = lse[:, start : start + HALF]
+
+    block(0, 1280, 256)
+    block(1, 1280, 256)
     finish_rows(0)
-    block(2, 1024, 512)
+    block(2, 1280, 256)
     finish_rows(1)
-    block(3, 1024, 512)
+    block(3, 1280, 256)
     finish_rows(2)
     peak = jnp.max(col_peak[...], axis=0, keepdims=True)
     total = jnp.sum(col_sum[...] * jnp.exp2(col_peak[...] - peak), axis=0, keepdims=True)
@@ -289,29 +291,30 @@
 
     for m in row_msgs:
         m.wait_recv()
-    stats = row_stats[:, 0:32, :]
+    stats = row_stats[...]
+    lane = lax.broadcasted_iota(jnp.int32, (16, 128), 1)
     peak = jnp.max(stats, axis=0)
     lse = peak + jnp.log(jnp.sum(jnp.exp2(stats - peak[None]), axis=0)) * (1.0 / LN2)
     row_lse[...] = lse
-    lane = lax.broadcasted_iota(jnp.int32, (32, 128), 1)
-    share = jnp.sum(jnp.where(lane < HALF, lse, 0.0).reshape(4, 8, 128), axis=0)
+    share = jnp.sum(jnp.where(lane < OWN, lse, 0.0).reshape(2, 8, 128), axis=0)
+    for i in range(3):
+        pair_all[:, pl.ds(32 * i, 32)] = stats[:, i, OWN:128]
     order[pl.ds(64, 64), :] = jnp.zeros((64, 128), f32)
     for b in range(8):
         p, half = b // 2, b % 2
         for q in range(4):
             at = piece(half, p, q)
-            order[pl.ds(4 * b + q, 1), :] = row_lse[pl.ds(half * 16 + at, 1), :]
-            order[pl.ds(32 + 4 * b + q, 1), :] = row_stats[at, pl.ds(32, 1), :]
+            order[pl.ds(4 * b + q, 1), :] = row_lse[pl.ds(at, 1), :]
+            order[pl.ds(32 + 4 * b + q, 1), :] = pair_all[pl.ds(at, 1), :]
     turned = order[...].T
     for b in range(8):
         half = b % 2
         for q in range(4):
             n = 4 * b + q
             rows = pl.ds(n * HALF, HALF)
-            row_rep[rows, :] = jnp.broadcast_to(turned[0:HALF, n : n + 1], (HALF, 128))
-            pair_rep[rows, :] = jnp.broadcast_to(
-                turned[half * HALF : (half + 1) * HALF, 32 + n : 33 + n], (HALF, 128)
-            )
+            mine = turned[half * HALF : (half + 1) * HALF, :]
+            row_rep[rows, :] = jnp.broadcast_to(mine[:, n : n + 1], (HALF, 128))
+            pair_rep[rows, :] = jnp.broadcast_to(mine[:, 32 + n : 33 + n], (HALF, 128))
 
     for m in col_msgs:
         m.wait_recv()
@@ -319,7 +322,6 @@
     peak = jnp.max(stats, axis=0)
     lse = peak + jnp.log(jnp.sum(jnp.exp2(stats - peak[None]), axis=0)) * (1.0 / LN2)
     col_lse[...] = lse
-    lane = lax.broadcasted_iota(jnp.int32, (16, 128), 1)
     share = share + jnp.sum(jnp.where(lane < OWN, lse, 0.0).reshape(2, 8, 128), axis=0)
     col_rep[...] = jnp.concatenate(
         [col_lse[pl.ds(owner(pos, rel), 1), :][:, 0:OWN] for pos in range(8) for rel in (0, 1)], axis=1
@@ -533,33 +535,33 @@
     for k in (0, 1):
         weigh(0, k)
     near_send()
+    finish = total_along(share * (1.0 / 16.0) - 2.0 * positive[...], "dz", 8)
     add_sibling(5, 6)
     z_near(3, 0)
     z_near(3, 1)
-    finish = total_along(share * (1.0 / 16.0) - 2.0 * positive[...], "dx", 4)
     passage_term(1)
     sib_send(1)
     near_terms(1)
+    finish = total_along(finish(), "dx", 4)
     far_wait()
     rest_encode()
     rest_send()
     add_sibling(3, 4)
     z_near(2, 0)
-    finish = total_along(finish(), "dy", 4)
     passage_term(0)
     sib_send(0)
+    finish = total_along(finish(), "dy", 4)
     z_near(2, 1)
     query_term(0)
+    finish = total_along(finish(), "dc", 2)
     near_add()
     rest_add(0)
     last_send(3, 1)
-    finish = total_along(finish(), "dz", 8)
     add_sibling(1, 2, 0)
     z_near(1, 0)
     rest_add(1)
     last_send(2)
     z_near(1, 1)
-    finish = total_along(finish(), "dc", 2)
     total = finish()
     loss_out[...] = jnp.sum(jnp.sum(total, axis=1, keepdims=True), axis=0, keepdims=True) * (LN2 / (2.0 * PAIRS))
     query_out()
@@ -590,9 +592,10 @@
             pltpu.VMEM((ROWS, 128), f32),
             pltpu.VMEM((8, ROWS), f32),
             pltpu.VMEM((8, ROWS), f32),
-            pltpu.VMEM((16, 40, 128), f32),
             pltpu.VMEM((16, 16, 128), f32),
-            pltpu.VMEM((32, 128), f32),
+            pltpu.VMEM((16, 16, 128), f32),
+            pltpu.VMEM((16, 128), f32),
+            pltpu.VMEM((16, 128), f32),
             pltpu.VMEM((ROWS, 128), f32),
             pltpu.VMEM((ROWS, 128), f32),
             pltpu.VMEM((128, 128), f32),

time: 81.1 us -> 79.2 us (0.977); the launches traced: 79.9 us -> 79.1 us
    pallas_call x1, Pallas kernels: 76.2 us -> 75.4 us  [on_device(): pl.pallas_call(kernel, out_shape=(pltpu.VMEM((OWN, D), bf16), pltpu.VMEM(...]
where the time goes in v2:
time: 79.2 us; the launch traced here: 79.1 us
  Pallas kernels  75.4 us (95%)
  between operations  2.33 us (3%)
  local copies, waits for them, and re-layouts  1.36 us (2%)
    pallas_call x1, Pallas kernels, on_device(): pl.pallas_call(kernel, out_shape=(pltpu.VMEM((OWN, D), bf16), pltpu.VMEM(...  75.4 us

profile of v2, /device:TPU:2, one launch (start us, length us, event | category | flops | bytes accessed | tf_op | source)
XLA Modules:
  0.0 79.1 jit_solution(8617331484400084601)
XLA Ops:
  0.6 75.4 %shard_map.58 = (bf16[96,1024]{1,0:T(8,128)(2,1)S(1)}, bf16[96,1024]{1,0:T(8,128)(2,1)S(1)}, f32[1,1]{1,0:T(1,128)}) custom-call(bf16[96,1024]{1,0:T(8,128)(2,1)} %q_in.1, bf16[96,1024]{1,0:T(8,128)(2,1)} %p_in.1, s32[1,96]{1,0:T(1,128)} %bitcast.2), custom_call_target="tpu_custom_call" | custom-call | tf_op jit(solution)/shard_map/pallas_call | solution.py:576
  76.0 0.7 copy.9
  76.7 0.7 copy.10

commit v3 on v2

--- a/solution.py
+++ b/solution.py
@@ -190,8 +190,9 @@
         spread(half, 3)
     z_pass(2, 0)
 
-    def block(p, start, width):
-        rows = pl.ds(p * CHUNK, CHUNK)
+    def block(p, start, width, chunks=1):
+        height = chunks * CHUNK
+        rows = pl.ds(p * CHUNK, height)
         cols = pl.ds(start, width)
         s = lax.dot_general(
             q_all[rows, :], p_all[cols, :], (((1,), (1,)), ((), ())), preferred_element_type=f32
@@ -205,7 +206,7 @@
             total += jnp.exp2(part - peak)
         row_peak[rows, :] = peak
         row_sum[rows, :] = total
-        s3 = s.reshape(CHUNK // 8, 8, width)
+        s3 = s.reshape(height // 8, 8, width)
         old = col_peak[:, cols]
         peak = jnp.maximum(old, jnp.max(s3, axis=0))
         col_sum[:, cols] = col_sum[:, cols] * jnp.exp2(old - peak) + jnp.sum(jnp.exp2(s3 - peak[None]), axis=0)
@@ -258,13 +259,9 @@
                 start = half * BUNDLE + q * HALF
                 row_stats[slot, pl.ds(piece(half, p, q), 1), pl.ds(half * HALF, HALF)] = lse[:, start : start + HALF]
 
-    block(0, 1280, 256)
-    block(1, 1280, 256)
-    finish_rows(0)
-    block(2, 1280, 256)
-    finish_rows(1)
-    block(3, 1280, 256)
-    finish_rows(2)
+    block(0, 1280, 256, 4)
+    for p in range(3):
+        finish_rows(p)
     peak = jnp.max(col_peak[...], axis=0, keepdims=True)
     total = jnp.sum(col_sum[...] * jnp.exp2(col_peak[...] - peak), axis=0, keepdims=True)
     lse = peak + jnp.log(total) * (1.0 / LN2)

time: 79.2 us -> 80.4 us (1.015)
  Pallas kernels: 75.4 us -> 76.6 us
    pallas_call x1, Pallas kernels: 75.4 us -> 76.6 us  [on_device(): pl.pallas_call(kernel, out_shape=(pltpu.VMEM((OWN, D), bf16), pltpu.VMEM(...]
where the time goes in v3:
time: 80.4 us; the launch traced here: 80.3 us
  Pallas kernels  76.6 us (95%)
  between operations  2.33 us (3%)
  local copies, waits for them, and re-layouts  1.36 us (2%)
    pallas_call x1, Pallas kernels, on_device(): pl.pallas_call(kernel, out_shape=(pltpu.VMEM((OWN, D), bf16), pltpu.VMEM(...  76.6 us

profile of v3, /device:TPU:2, one launch (start us, length us, event | category | flops | bytes accessed | tf_op | source)
XLA Modules:
  0.0 80.3 jit_solution(16681693115468767266)
XLA Ops:
  0.6 76.6 %shard_map.58 = (bf16[96,1024]{1,0:T(8,128)(2,1)S(1)}, bf16[96,1024]{1,0:T(8,128)(2,1)S(1)}, f32[1,1]{1,0:T(1,128)}) custom-call(bf16[96,1024]{1,0:T(8,128)(2,1)} %q_in.1, bf16[96,1024]{1,0:T(8,128)(2,1)} %p_in.1, s32[1,96]{1,0:T(1,128)} %bitcast.2), custom_call_target="tpu_custom_call" | custom-call | tf_op jit(solution)/shard_map/pallas_call | solution.py:573
  77.3 0.7 copy.9
  77.9 0.7 copy.10
